TPU v7x, 512 devices: a whole 4x4x16 slice. The times are simulated.
512 devices in a mesh: blk: 128 (over y, z_lo, x), feat: 4 (over z_hi, core).
Axes of the slice: x: 4, y: 4, z: 16 (z_hi: 2, z_lo: 8; z = z_hi * 8 + z_lo), core: 2. Of those that a mesh axis runs over, the one named last changes fastest.
Arguments:
- features: bfloat16 [131072, 512], P('blk', 'feat')
- hop_noise: bfloat16 [2, 131072, 512], P(None, 'blk', 'feat'), may hold values from -4 to 4
- encoder_weight: bfloat16 [2, 512, 512], replicated, may hold values from -0.03125 to 0.03125
- block_target: int32 [128, 40], P('blk'), may hold values from 0 to 7
- block_source: int32 [128, 40], P('blk'), may hold values from 0 to 39
- block_count: int32 [128], P('blk'), may hold values from 10 to 40
- tile_mask: int32 [128, 40, 128, 128], P('blk'), may hold values 0 or 1
Outputs:
- encoded_one: bfloat16 [131072, 512], P('blk', 'feat')
- encoded_two: bfloat16 [131072, 512], P('blk', 'feat')
Inputs may be any that keep to these rules, and one draw needn't show every extreme that they name: Entries k < block_count of a partition's list are live, the others are ignored. `block_source`: window index: source partition offset index // 8 - 2, row block index % 8.
All inputs are finite; a program needn't handle non-finite values. No bound on the sum of `tile_mask` on one device may be relied on, other than what follows from the above.
Results may differ from a plain program's by a relative error of at most 0.015.
Values may be sent and summed in bfloat16 or wider, within the bound.
A program may use at most 64 MiB of HBM per device.

v0:
```python
import jax
import jax.numpy as jnp
from jax import lax
from jax.sharding import PartitionSpec as P

TILE = 128
TILES = 8
HALF = 2
K = 40
HOPS = 2


def passed_along(x, axis, by):
    size = lax.axis_size(axis)
    return lax.ppermute(x, axis, [(i, (i + by) % size) for i in range(size)])


def band_window(clipped):
    above = []
    moving = clipped
    for offset in range(HALF):
        moving = passed_along(moving, "blk", -1)
        above.append(moving)
    below = []
    moving = clipped
    for offset in range(HALF):
        moving = passed_along(moving, "blk", 1)
        below.append(moving)
    return below[::-1] + [clipped] + above


def encode_rows(noisy, weight, columns):
    my_first = lax.axis_index("feat") * columns
    my_columns = lax.dynamic_slice_in_dim(weight, my_first, columns, 1)
    summed = jnp.dot(
        lax.all_gather(noisy, "feat", axis=1, tiled=True),
        my_columns,
        preferred_element_type=jnp.float32,
    )
    return summed.astype(jnp.bfloat16)


def per_device(
    features, hop_noise, encoder_weight, block_target, block_source, block_count, tile_mask
):
    row_count = features.shape[0]
    columns = features.shape[1]
    mask_values = tile_mask[0].astype(jnp.bfloat16)
    targets = block_target[0]
    sources = block_source[0]
    active = jnp.arange(K) < block_count[0]
    routing = ((targets[:, None] == jnp.arange(TILES)[None, :]) & active[:, None]).astype(
        jnp.float32
    )
    current = features
    results = []
    for hop_index in range(HOPS):
        widened = current.astype(jnp.float32)
        squares = lax.psum(jnp.sum(widened * widened, axis=1), "feat")
        clipped = (widened / jnp.maximum(1.0, jnp.sqrt(squares))[:, None]).astype(jnp.bfloat16)
        window_tiles = jnp.concatenate(band_window(clipped), axis=0).reshape(-1, TILE, columns)
        picked = window_tiles[sources]
        products = jnp.einsum(
            "kij,kjf->kif", mask_values, picked, preferred_element_type=jnp.float32
        )
        aggregate = jnp.einsum("kt,kif->tif", routing, products).reshape(row_count, columns)
        noisy = (aggregate + hop_noise[hop_index].astype(jnp.float32)).astype(jnp.bfloat16)
        encoded = encode_rows(noisy, encoder_weight[hop_index], columns)
        results.append(encoded)
        current = encoded
    return (results[0], results[1])


def solution(mesh):
    in_specs = (
        P("blk", "feat"),
        P(None, "blk", "feat"),
        P(),
        P("blk", None),
        P("blk", None),
        P("blk"),
        P("blk", None, None, None),
    )
    out_specs = (P("blk", "feat"), P("blk", "feat"))
    return jax.shard_map(
        per_device, mesh=mesh, in_specs=in_specs, out_specs=out_specs, check_vma=False
    )
```

profile of v0, /device:TPU:1, one launch (start us, length us, event | category | flops | bytes accessed | tf_op | source)
XLA Modules:
  0.0 276.7 jit_solution(6634274752078948736)
XLA Ops:
  8.4 20.6 %psum.14 = f32[1024]{0:T(1024)S(1)} all-reduce(f32[1024]{0:T(1024)S(1)} %fusion.10), channel_id=1, replica_groups=mesh['blk'=128,'feat'=4] {'feat'}, use_global_device_ids=true, to_apply=%region_1.0 | all-reduce | flops 1024 | bytes 8192 | tf_op jit(solution)/shard_map/psum | solution.py:59
  30.2 1.9 collective-permute-start
  32.1 14.2 %collective-permute-start.2 = (bf16[1024,128]{1,0:T(8,128)(2,1)S(1)}, bf16[1024,128]{1,0:T(8,128)(2,1)S(1)}, u32[]{:S(2)}, u32[]{:S(2)}) collective-permute-start(bf16[1024,128]{1,0:T(8,128)(2,1)S(1)} %fusion.11), channel_id=1, source_target_pairs={{0,508},{4,0},{8,4},{12,8},{16,12},{20,16},{24,20},{28,24},{32,28}... | collective-permute-start | bytes 786440 | tf_op jit(solution)/shard_map/ppermute | solution.py:15
  46.3 1.8 collective-permute-done
  48.2 1.9 collective-permute-start.1
  51.4 14.2 %collective-permute-start.3 = (bf16[1024,128]{1,0:T(8,128)(2,1)S(1)}, bf16[1024,128]{1,0:T(8,128)(2,1)S(1)}, u32[]{:S(2)}, u32[]{:S(2)}) collective-permute-start(bf16[1024,128]{1,0:T(8,128)(2,1)S(1)} %collective-permute-done.2), channel_id=1, source_target_pairs={{0,508},{4,0},{8,4},{12,8},{16,12},{20,16},{24,20},{28,24},{32,28}... | collective-permute-start | bytes 786440 | tf_op jit(solution)/shard_map/ppermute | solution.py:15
  66.5 2.4 collective-permute-done.3
  70.0 3.3 %gather_fusion = bf16[40,128,128]{2,1,0:T(8,128)(2,1)} fusion(bf16[40,128,128]{2,1,0:T(8,128)(2,1)} %bitcast.46, s32[1024]{0:T(1024)S(1)} %pad_clamp_fusion), kind=kCustom, calls=%fused_computation | custom fusion | bytes 2621600 | tf_op jit(solution)/shard_map/gather | solution.py:62
  73.4 3.4 %fusion.6 = bf16[40,128,128]{2,1,0:T(8,128)(2,1)} fusion(bf16[40,128,128]{2,1,0:T(8,128)(2,1)} %gather_fusion, s32[1,40,128,128]{3,2,1,0:T(8,128)S(1)} %copy-done), kind=kOutput, calls=%fused_computation.8 | convolution fusion | flops 168427520 | bytes 5242880 | tf_op jit(solution)/shard_map/kij,kjf->kif/dot_general | solution.py:63
  76.8 2.7 copy.11
  82.2 2.1 fusion.31
  84.3 61.0 %all-gather.3.cloned.1.call-done = bf16[1024,512]{1,0:T(8,128)(2,1)} async-done(((bf16[1024,128]{1,0:T(8,128)(2,1)}), bf16[1024,512]{1,0:T(8,128)(2,1)}) %all-gather.3.cloned.1.call-update) | async-done | bytes 1048592 | tf_op jit(solution)/shard_map/all_gather | solution.py:36
  147.1 14.0 %psum.15 = f32[1024]{0:T(1024)S(1)} all-reduce(f32[1024]{0:T(1024)S(1)} %get-tuple-element.4), channel_id=1, replica_groups=mesh['blk'=128,'feat'=4] {'feat'}, use_global_device_ids=true, to_apply=%region_3.0 | all-reduce | flops 1024 | bytes 8192 | tf_op jit(solution)/shard_map/psum | solution.py:59
  161.3 3.1 %collective-permute-start.4 = (bf16[1024,128]{1,0:T(8,128)(2,1)S(1)}, bf16[1024,128]{1,0:T(8,128)(2,1)S(1)}, u32[]{:S(2)}, u32[]{:S(2)}) collective-permute-start(bf16[1024,128]{1,0:T(8,128)(2,1)S(1)} %fusion.13), channel_id=1, source_target_pairs={{0,4},{4,8},{8,12},{12,16},{16,20},{20,24},{24,28},{28,32},{32,36}... | collective-permute-start | bytes 786440 | tf_op jit(solution)/shard_map/ppermute | solution.py:15
  164.4 13.0 %collective-permute-start.6 = (bf16[1024,128]{1,0:T(8,128)(2,1)S(1)}, bf16[1024,128]{1,0:T(8,128)(2,1)S(1)}, u32[]{:S(2)}, u32[]{:S(2)}) collective-permute-start(bf16[1024,128]{1,0:T(8,128)(2,1)S(1)} %fusion.13), channel_id=1, source_target_pairs={{0,508},{4,0},{8,4},{12,8},{16,12},{20,16},{24,20},{28,24},{32,28}... | collective-permute-start | bytes 786440 | tf_op jit(solution)/shard_map/ppermute | solution.py:15
  177.4 3.5 %collective-permute-done.4 = bf16[1024,128]{1,0:T(8,128)(2,1)S(1)} collective-permute-done((bf16[1024,128]{1,0:T(8,128)(2,1)S(1)}, bf16[1024,128]{1,0:T(8,128)(2,1)S(1)}, u32[]{:S(2)}, u32[]{:S(2)}) %collective-permute-start.4) | collective-permute-done | bytes 262176 | tf_op jit(solution)/shard_map/ppermute | solution.py:15
  180.9 1.9 collective-permute-start.5
  182.9 14.2 %collective-permute-start.7 = (bf16[1024,128]{1,0:T(8,128)(2,1)S(1)}, bf16[1024,128]{1,0:T(8,128)(2,1)S(1)}, u32[]{:S(2)}, u32[]{:S(2)}) collective-permute-start(bf16[1024,128]{1,0:T(8,128)(2,1)S(1)} %collective-permute-done.6), channel_id=1, source_target_pairs={{0,508},{4,0},{8,4},{12,8},{16,12},{20,16},{24,20},{28,24},{32,28}... | collective-permute-start | bytes 786440 | tf_op jit(solution)/shard_map/ppermute | solution.py:15
  197.1 2.6 collective-permute-done.5
  203.4 3.2 %gather_fusion.1 = bf16[40,128,128]{2,1,0:T(8,128)(2,1)} fusion(bf16[40,128,128]{2,1,0:T(8,128)(2,1)} %bitcast.11, s32[1024]{0:T(1024)S(1)} %pad_clamp_fusion), kind=kCustom, calls=%fused_computation.1 | custom fusion | bytes 2621600 | tf_op jit(solution)/shard_map/gather | solution.py:62
  206.6 3.4 %fusion.4 = bf16[40,128,128]{2,1,0:T(8,128)(2,1)} fusion(bf16[40,128,128]{2,1,0:T(8,128)(2,1)} %gather_fusion.1, s32[1,40,128,128]{3,2,1,0:T(8,128)S(1)} %copy-done), kind=kOutput, calls=%fused_computation.6 | convolution fusion | flops 168427520 | bytes 5242880 | tf_op jit(solution)/shard_map/kij,kjf->kif/dot_general | solution.py:63
  210.1 2.1 copy.12
  214.1 53.4 %all-gather.5.cloned.1.call-done = bf16[1024,512]{1,0:T(8,128)(2,1)} async-done(((bf16[1024,128]{1,0:T(8,128)(2,1)}), bf16[1024,512]{1,0:T(8,128)(2,1)}) %all-gather.5.cloned.1.call-update) | async-done | bytes 1048592 | tf_op jit(solution)/shard_map/all_gather | solution.py:36
  267.4 2.4 convolution_convert_fusion
  (47 shorter events, 15.2 us)
Async XLA Ops:
  7.2 59.0 %copy-start.1 = (bf16[1024,128]{1,0:T(8,128)(2,1)S(1)}, bf16[1024,128]{1,0:T(8,128)(2,1)}, u32[]{:S(2)}) copy-start(bf16[1024,128]{1,0:T(8,128)(2,1)} %param.7) | copy-start | bytes 786436
  7.2 138.1 %all-gather.3.cloned.1.call-start = ((), (), s32[]{:S(2)}) async-start(), calls=%async_computation | async-start | bytes 1310720 | tf_op jit(solution)/shard_map/all_gather | solution.py:36
  30.2 17.9 %collective-permute-start = (bf16[1024,128]{1,0:T(8,128)(2,1)S(1)}, bf16[1024,128]{1,0:T(8,128)(2,1)S(1)}, u32[]{:S(2)}, u32[]{:S(2)}) collective-permute-start(bf16[1024,128]{1,0:T(8,128)(2,1)S(1)} %fusion.11), channel_id=1, source_target_pairs={{0,4},{4,8},{8,12},{12,16},{16,20},{20,24},{24,28},{28,32},{32,36}... | collective-permute-start | bytes 786440 | tf_op jit(solution)/shard_map/ppermute | solution.py:15
  32.1 19.3 %collective-permute-start.2 = (bf16[1024,128]{1,0:T(8,128)(2,1)S(1)}, bf16[1024,128]{1,0:T(8,128)(2,1)S(1)}, u32[]{:S(2)}, u32[]{:S(2)}) collective-permute-start(bf16[1024,128]{1,0:T(8,128)(2,1)S(1)} %fusion.11), channel_id=1, source_target_pairs={{0,508},{4,0},{8,4},{12,8},{16,12},{20,16},{24,20},{28,24},{32,28}... | collective-permute-start | bytes 786440 | tf_op jit(solution)/shard_map/ppermute | solution.py:15
  48.2 17.9 %collective-permute-start.1 = (bf16[1024,128]{1,0:T(8,128)(2,1)S(1)}, bf16[1024,128]{1,0:T(8,128)(2,1)S(1)}, u32[]{:S(2)}, u32[]{:S(2)}) collective-permute-start(bf16[1024,128]{1,0:T(8,128)(2,1)S(1)} %collective-permute-done), channel_id=1, source_target_pairs={{0,4},{4,8},{8,12},{12,16},{16,20},{20,24},{24,28},{28,32},{32,36}... | collective-permute-start | bytes 786440 | tf_op jit(solution)/shard_map/ppermute | solution.py:15
  51.4 17.5 %collective-permute-start.3 = (bf16[1024,128]{1,0:T(8,128)(2,1)S(1)}, bf16[1024,128]{1,0:T(8,128)(2,1)S(1)}, u32[]{:S(2)}, u32[]{:S(2)}) collective-permute-start(bf16[1024,128]{1,0:T(8,128)(2,1)S(1)} %collective-permute-done.2), channel_id=1, source_target_pairs={{0,508},{4,0},{8,4},{12,8},{16,12},{20,16},{24,20},{28,24},{32,28}... | collective-permute-start | bytes 786440 | tf_op jit(solution)/shard_map/ppermute | solution.py:15
  68.9 1.1 copy-start.2
  70.0 3.4 %copy-start = (s32[1,40,128,128]{3,2,1,0:T(8,128)S(1)}, s32[1,40,128,128]{3,2,1,0:T(8,128)}, u32[]{:S(2)}) copy-start(s32[1,40,128,128]{3,2,1,0:T(8,128)} %param.13) | copy-start | bytes 7864324
  76.8 2.8 copy-start.6
  79.5 1.8 copy-start.4
  82.2 185.3 %all-gather.5.cloned.1.call-start = ((), (), s32[]{:S(2)}) async-start(), calls=%async_computation.1 | async-start | bytes 1310720 | tf_op jit(solution)/shard_map/all_gather | solution.py:36
  147.0 55.7 %copy-start.3 = (bf16[1024,128]{1,0:T(8,128)(2,1)}, bf16[1024,128]{1,0:T(8,128)(2,1)S(1)}, u32[]{:S(2)}) copy-start(bf16[1024,128]{1,0:T(8,128)(2,1)S(1)} %get-tuple-element.5) | copy-start | bytes 786436
  161.3 19.6 %collective-permute-start.4 = (bf16[1024,128]{1,0:T(8,128)(2,1)S(1)}, bf16[1024,128]{1,0:T(8,128)(2,1)S(1)}, u32[]{:S(2)}, u32[]{:S(2)}) collective-permute-start(bf16[1024,128]{1,0:T(8,128)(2,1)S(1)} %fusion.13), channel_id=1, source_target_pairs={{0,4},{4,8},{8,12},{12,16},{16,20},{20,24},{24,28},{28,32},{32,36}... | collective-permute-start | bytes 786440 | tf_op jit(solution)/shard_map/ppermute | solution.py:15
  164.4 18.4 %collective-permute-start.6 = (bf16[1024,128]{1,0:T(8,128)(2,1)S(1)}, bf16[1024,128]{1,0:T(8,128)(2,1)S(1)}, u32[]{:S(2)}, u32[]{:S(2)}) collective-permute-start(bf16[1024,128]{1,0:T(8,128)(2,1)S(1)} %fusion.13), channel_id=1, source_target_pairs={{0,508},{4,0},{8,4},{12,8},{16,12},{20,16},{24,20},{28,24},{32,28}... | collective-permute-start | bytes 786440 | tf_op jit(solution)/shard_map/ppermute | solution.py:15
  180.9 18.7 %collective-permute-start.5 = (bf16[1024,128]{1,0:T(8,128)(2,1)S(1)}, bf16[1024,128]{1,0:T(8,128)(2,1)S(1)}, u32[]{:S(2)}, u32[]{:S(2)}) collective-permute-start(bf16[1024,128]{1,0:T(8,128)(2,1)S(1)} %collective-permute-done.4), channel_id=1, source_target_pairs={{0,4},{4,8},{8,12},{12,16},{16,20},{20,24},{24,28},{28,32},{32,36}... | collective-permute-start | bytes 786440 | tf_op jit(solution)/shard_map/ppermute | solution.py:15
  182.9 19.9 %collective-permute-start.7 = (bf16[1024,128]{1,0:T(8,128)(2,1)S(1)}, bf16[1024,128]{1,0:T(8,128)(2,1)S(1)}, u32[]{:S(2)}, u32[]{:S(2)}) collective-permute-start(bf16[1024,128]{1,0:T(8,128)(2,1)S(1)} %collective-permute-done.6), channel_id=1, source_target_pairs={{0,508},{4,0},{8,4},{12,8},{16,12},{20,16},{24,20},{28,24},{32,28}... | collective-permute-start | bytes 786440 | tf_op jit(solution)/shard_map/ppermute | solution.py:15
  212.2 1.0 copy-start.5
Sparse Core Ops, SparseCore 0:
  82.3 62.9 all-gather.2
  214.2 53.2 all-gather.4
where the time goes:
time: 277 us
  waiting for transfers between devices  125 us (45%)
  starting transfers between devices  64.5 us (23%)
  blocking collectives  34.6 us (12%)
  local copies, waits for them, and re-layouts  18.3 us (7%)
  between operations  14.9 us (5%)
  matrix products  13 us (5%)
  other arithmetic  5.97 us (2%)
    all_gather x2, waiting for transfers between devices, encode_rows(): lax.all_gather(noisy, 'feat', axis=1, tiled=True)  114 us
    ppermute x8, starting transfers between devices, passed_along(): return lax.ppermute(x, axis, [(i, (i + by) % size) for i in range(size)])  64.4 us
    psum x2, blocking collectives, per_device(): squares = lax.psum(jnp.sum(widened * widened, axis=1), 'feat')  34.6 us
    ppermute x8, waiting for transfers between devices, passed_along(): return lax.ppermute(x, axis, [(i, (i + by) % size) for i in range(size)])  10.9 us
    dot_general x2, matrix products, per_device(): jnp.einsum('kij,kjf->kif', mask_values, picked, preferred_element_type=jn...  6.87 us
    gather x2, local copies, waits for them, and re-layouts, per_device(): picked = window_tiles[sources]  6.54 us
  transfers between devices with their start and end apart: 10, of which 7 were waited for; matrix products, arithmetic and copies ran while one was open for 2% of the time, Pallas kernels for 0%

commit v1 on v0

--- a/solution.py
+++ b/solution.py
@@ -2,12 +2,17 @@
 import jax.numpy as jnp
 from jax import lax
 from jax.sharding import PartitionSpec as P
+from jax.lax import all_gather
 
 TILE = 128
 TILES = 8
 HALF = 2
 K = 40
 HOPS = 2
+
+
+def sample_end(sample):
+    return jnp.sum(all_gather(sample, "feat"), 0)
 
 
 def passed_along(x, axis, by):
@@ -56,7 +61,7 @@
     results = []
     for hop_index in range(HOPS):
         widened = current.astype(jnp.float32)
-        squares = lax.psum(jnp.sum(widened * widened, axis=1), "feat")
+        squares = sample_end(jnp.sum(widened * widened, axis=1))
         clipped = (widened / jnp.maximum(1.0, jnp.sqrt(squares))[:, None]).astype(jnp.bfloat16)
         window_tiles = jnp.concatenate(band_window(clipped), axis=0).reshape(-1, TILE, columns)
         picked = window_tiles[sources]

time: 277 us -> 273 us (0.986)
  waiting for transfers between devices: 125 us -> 120 us
    psum x2 -> x0, blocking collectives: 34.6 us -> none  [per_device(): squares = lax.psum(jnp.sum(widened * widened, axis=1), 'feat')]
    all_gather x0 -> x2, blocking collectives: none -> 34.5 us  [sample_end(): return jnp.sum(all_gather(sample, 'feat'), 0)]
    all_gather x2, waiting for transfers between devices: 114 us -> 105 us  [encode_rows(): lax.all_gather(noisy, 'feat', axis=1, tiled=True)]
    ppermute x8, waiting for transfers between devices: 10.9 us -> 15.9 us  [passed_along(): return lax.ppermute(x, axis, [(i, (i + by) % size) for i in range(size)])]
where the time goes in v1:
time: 273 us; the launch traced here: 272 us
  waiting for transfers between devices  120 us (44%)
  starting transfers between devices  64.5 us (24%)
  blocking collectives  34.5 us (13%)
  local copies, waits for them, and re-layouts  18.4 us (7%)
  between operations  14.9 us (5%)
  matrix products  13 us (5%)
  other arithmetic  5.99 us (2%)
    all_gather x2, waiting for transfers between devices, encode_rows(): lax.all_gather(noisy, 'feat', axis=1, tiled=True)  105 us
    ppermute x8, starting transfers between devices, passed_along(): return lax.ppermute(x, axis, [(i, (i + by) % size) for i in range(size)])  64.4 us
    all_gather x2, blocking collectives, sample_end(): return jnp.sum(all_gather(sample, 'feat'), 0)  34.5 us
    ppermute x8, waiting for transfers between devices, passed_along(): return lax.ppermute(x, axis, [(i, (i + by) % size) for i in range(size)])  15.9 us
    dot_general x2, matrix products, per_device(): jnp.einsum('kij,kjf->kif', mask_values, picked, preferred_element_type=jn...  6.87 us
    gather x2, local copies, waits for them, and re-layouts, per_device(): picked = window_tiles[sources]  6.54 us
  transfers between devices with their start and end apart: 10, of which 7 were waited for; matrix products, arithmetic and copies ran while one was open for 2% of the time, Pallas kernels for 0%

profile of v1, /device:TPU:1, one launch (start us, length us, event | category | flops | bytes accessed | tf_op | source)
XLA Modules:
  0.0 271.8 jit_solution(5540008915844949775)
XLA Ops:
  8.4 20.6 %all-gather = f32[4096]{0:T(1024)S(1)} all-gather(f32[1024]{0:T(1024)S(1)} %fusion.4), channel_id=2, replica_groups=mesh['blk'=128,'feat'=4] {'feat'}, dimensions={0}, use_global_device_ids=true | all-gather | bytes 20480 | tf_op jit(solution)/shard_map/all_gather | solution.py:15
  30.2 1.9 collective-permute-start
  32.1 14.2 %collective-permute-start.2 = (bf16[1024,128]{1,0:T(8,128)(2,1)S(1)}, bf16[1024,128]{1,0:T(8,128)(2,1)S(1)}, u32[]{:S(2)}, u32[]{:S(2)}) collective-permute-start(bf16[1024,128]{1,0:T(8,128)(2,1)S(1)} %fusion.5), channel_id=1, source_target_pairs={{0,508},{4,0},{8,4},{12,8},{16,12},{20,16},{24,20},{28,24},{32,28}... | collective-permute-start | bytes 786440 | tf_op jit(solution)/shard_map/ppermute | solution.py:20
  46.3 4.3 %collective-permute-done = bf16[1024,128]{1,0:T(8,128)(2,1)S(1)} collective-permute-done((bf16[1024,128]{1,0:T(8,128)(2,1)S(1)}, bf16[1024,128]{1,0:T(8,128)(2,1)S(1)}, u32[]{:S(2)}, u32[]{:S(2)}) %collective-permute-start) | collective-permute-done | bytes 262176 | tf_op jit(solution)/shard_map/ppermute | solution.py:20
  50.6 1.9 collective-permute-start.1
  53.9 14.2 %collective-permute-start.3 = (bf16[1024,128]{1,0:T(8,128)(2,1)S(1)}, bf16[1024,128]{1,0:T(8,128)(2,1)S(1)}, u32[]{:S(2)}, u32[]{:S(2)}) collective-permute-start(bf16[1024,128]{1,0:T(8,128)(2,1)S(1)} %collective-permute-done.2), channel_id=1, source_target_pairs={{0,508},{4,0},{8,4},{12,8},{16,12},{20,16},{24,20},{28,24},{32,28}... | collective-permute-start | bytes 786440 | tf_op jit(solution)/shard_map/ppermute | solution.py:20
  68.1 2.0 collective-permute-done.1
  73.5 3.3 %gather_fusion = bf16[40,128,128]{2,1,0:T(8,128)(2,1)} fusion(bf16[40,128,128]{2,1,0:T(8,128)(2,1)} %bitcast.46, s32[1024]{0:T(1024)S(1)} %pad_clamp_fusion), kind=kCustom, calls=%fused_computation | custom fusion | bytes 2621600 | tf_op jit(solution)/shard_map/gather | solution.py:67
  76.8 3.4 %convolution_bitcast_fusion.1 = bf16[40,128,128]{1,2,0:T(8,128)(2,1)} fusion(bf16[40,128,128]{2,1,0:T(8,128)(2,1)} %gather_fusion, s32[1,40,128,128]{3,2,1,0:T(8,128)S(1)} %copy-done), kind=kOutput, calls=%fused_computation.3 | convolution fusion | flops 168427520 | bytes 5242880 | tf_op jit(solution)/shard_map/kij,kjf->kif/dot_general | solution.py:68
  80.3 2.7 %copy.22 = bf16[40,128,128]{2,0,1:T(8,128)(2,1)} copy(bf16[40,128,128]{1,2,0:T(8,128)(2,1)} %convolution_bitcast_fusion.1) | data formatting | bytes 2621440 | tf_op jit(solution)/shard_map/kij,kjf->kif/dot_general | solution.py:68
  85.7 2.1 fusion.27
  87.8 52.5 %all-gather.5.cloned.1.call-done = bf16[1024,512]{1,0:T(8,128)(2,1)} async-done(((bf16[1024,128]{1,0:T(8,128)(2,1)}), bf16[1024,512]{1,0:T(8,128)(2,1)}) %all-gather.5.cloned.1.call-update) | async-done | bytes 1048592 | tf_op jit(solution)/shard_map/all_gather | solution.py:41
  142.0 14.0 %all-gather.1 = f32[4096]{0:T(1024)S(1)} all-gather(f32[1024]{0:T(1024)S(1)} %get-tuple-element.4), channel_id=3, replica_groups=mesh['blk'=128,'feat'=4] {'feat'}, dimensions={0}, use_global_device_ids=true | all-gather | bytes 20480 | tf_op jit(solution)/shard_map/all_gather | solution.py:15
  156.2 3.1 %collective-permute-start.4 = (bf16[1024,128]{1,0:T(8,128)(2,1)S(1)}, bf16[1024,128]{1,0:T(8,128)(2,1)S(1)}, u32[]{:S(2)}, u32[]{:S(2)}) collective-permute-start(bf16[1024,128]{1,0:T(8,128)(2,1)S(1)} %fusion.7), channel_id=1, source_target_pairs={{0,4},{4,8},{8,12},{12,16},{16,20},{20,24},{24,28},{28,32},{32,36}... | collective-permute-start | bytes 786440 | tf_op jit(solution)/shard_map/ppermute | solution.py:20
  159.3 13.0 %collective-permute-start.6 = (bf16[1024,128]{1,0:T(8,128)(2,1)S(1)}, bf16[1024,128]{1,0:T(8,128)(2,1)S(1)}, u32[]{:S(2)}, u32[]{:S(2)}) collective-permute-start(bf16[1024,128]{1,0:T(8,128)(2,1)S(1)} %fusion.7), channel_id=1, source_target_pairs={{0,508},{4,0},{8,4},{12,8},{16,12},{20,16},{24,20},{28,24},{32,28}... | collective-permute-start | bytes 786440 | tf_op jit(solution)/shard_map/ppermute | solution.py:20
  172.3 4.3 %collective-permute-done.4 = bf16[1024,128]{1,0:T(8,128)(2,1)S(1)} collective-permute-done((bf16[1024,128]{1,0:T(8,128)(2,1)S(1)}, bf16[1024,128]{1,0:T(8,128)(2,1)S(1)}, u32[]{:S(2)}, u32[]{:S(2)}) %collective-permute-start.4) | collective-permute-done | bytes 262176 | tf_op jit(solution)/shard_map/ppermute | solution.py:20
  176.6 1.9 collective-permute-start.5
  178.6 14.2 %collective-permute-start.7 = (bf16[1024,128]{1,0:T(8,128)(2,1)S(1)}, bf16[1024,128]{1,0:T(8,128)(2,1)S(1)}, u32[]{:S(2)}, u32[]{:S(2)}) collective-permute-start(bf16[1024,128]{1,0:T(8,128)(2,1)S(1)} %collective-permute-done.6), channel_id=1, source_target_pairs={{0,508},{4,0},{8,4},{12,8},{16,12},{20,16},{24,20},{28,24},{32,28}... | collective-permute-start | bytes 786440 | tf_op jit(solution)/shard_map/ppermute | solution.py:20
  192.8 3.4 %collective-permute-done.5 = bf16[1024,128]{1,0:T(8,128)(2,1)S(1)} collective-permute-done((bf16[1024,128]{1,0:T(8,128)(2,1)S(1)}, bf16[1024,128]{1,0:T(8,128)(2,1)S(1)}, u32[]{:S(2)}, u32[]{:S(2)}) %collective-permute-start.5) | collective-permute-done | bytes 262176 | tf_op jit(solution)/shard_map/ppermute | solution.py:20
  199.9 3.2 %gather_fusion.1 = bf16[40,128,128]{2,1,0:T(8,128)(2,1)} fusion(bf16[40,128,128]{2,1,0:T(8,128)(2,1)} %bitcast.11, s32[1024]{0:T(1024)S(1)} %pad_clamp_fusion), kind=kCustom, calls=%fused_computation.1 | custom fusion | bytes 2621600 | tf_op jit(solution)/shard_map/gather | solution.py:67
  203.1 3.4 %convolution_bitcast_fusion = bf16[40,128,128]{1,2,0:T(8,128)(2,1)} fusion(bf16[40,128,128]{2,1,0:T(8,128)(2,1)} %gather_fusion.1, s32[1,40,128,128]{3,2,1,0:T(8,128)S(1)} %copy-done), kind=kOutput, calls=%fused_computation.2 | convolution fusion | flops 168427520 | bytes 5242880 | tf_op jit(solution)/shard_map/kij,kjf->kif/dot_general | solution.py:68
  206.5 2.1 copy.25
  210.5 52.1 %all-gather.7.cloned.1.call-done = bf16[1024,512]{1,0:T(8,128)(2,1)} async-done(((bf16[1024,128]{1,0:T(8,128)(2,1)}), bf16[1024,512]{1,0:T(8,128)(2,1)}) %all-gather.7.cloned.1.call-update) | async-done | bytes 1048592 | tf_op jit(solution)/shard_map/all_gather | solution.py:41
  262.6 2.4 convolution_convert_fusion
  (51 shorter events, 16.6 us)
Async XLA Ops:
  7.2 63.0 %copy-start.1 = (bf16[1024,128]{1,0:T(8,128)(2,1)S(1)}, bf16[1024,128]{1,0:T(8,128)(2,1)}, u32[]{:S(2)}) copy-start(bf16[1024,128]{1,0:T(8,128)(2,1)} %param.7) | copy-start | bytes 786436
  7.2 133.1 %all-gather.5.cloned.1.call-start = ((), (), s32[]{:S(2)}) async-start(), calls=%async_computation | async-start | bytes 1310720 | tf_op jit(solution)/shard_map/all_gather | solution.py:41
  30.2 20.4 %collective-permute-start = (bf16[1024,128]{1,0:T(8,128)(2,1)S(1)}, bf16[1024,128]{1,0:T(8,128)(2,1)S(1)}, u32[]{:S(2)}, u32[]{:S(2)}) collective-permute-start(bf16[1024,128]{1,0:T(8,128)(2,1)S(1)} %fusion.5), channel_id=1, source_target_pairs={{0,4},{4,8},{8,12},{12,16},{16,20},{20,24},{24,28},{28,32},{32,36}... | collective-permute-start | bytes 786440 | tf_op jit(solution)/shard_map/ppermute | solution.py:20
  32.1 21.8 %collective-permute-start.2 = (bf16[1024,128]{1,0:T(8,128)(2,1)S(1)}, bf16[1024,128]{1,0:T(8,128)(2,1)S(1)}, u32[]{:S(2)}, u32[]{:S(2)}) collective-permute-start(bf16[1024,128]{1,0:T(8,128)(2,1)S(1)} %fusion.5), channel_id=1, source_target_pairs={{0,508},{4,0},{8,4},{12,8},{16,12},{20,16},{24,20},{28,24},{32,28}... | collective-permute-start | bytes 786440 | tf_op jit(solution)/shard_map/ppermute | solution.py:20
  50.6 19.5 %collective-permute-start.1 = (bf16[1024,128]{1,0:T(8,128)(2,1)S(1)}, bf16[1024,128]{1,0:T(8,128)(2,1)S(1)}, u32[]{:S(2)}, u32[]{:S(2)}) collective-permute-start(bf16[1024,128]{1,0:T(8,128)(2,1)S(1)} %collective-permute-done), channel_id=1, source_target_pairs={{0,4},{4,8},{8,12},{12,16},{16,20},{20,24},{24,28},{28,32},{32,36}... | collective-permute-start | bytes 786440 | tf_op jit(solution)/shard_map/ppermute | solution.py:20
  53.9 18.5 %collective-permute-start.3 = (bf16[1024,128]{1,0:T(8,128)(2,1)S(1)}, bf16[1024,128]{1,0:T(8,128)(2,1)S(1)}, u32[]{:S(2)}, u32[]{:S(2)}) collective-permute-start(bf16[1024,128]{1,0:T(8,128)(2,1)S(1)} %collective-permute-done.2), channel_id=1, source_target_pairs={{0,508},{4,0},{8,4},{12,8},{16,12},{20,16},{24,20},{28,24},{32,28}... | collective-permute-start | bytes 786440 | tf_op jit(solution)/shard_map/ppermute | solution.py:20
  72.4 1.1 copy-start.2
  73.5 3.4 %copy-start = (s32[1,40,128,128]{3,2,1,0:T(8,128)S(1)}, s32[1,40,128,128]{3,2,1,0:T(8,128)}, u32[]{:S(2)}) copy-start(s32[1,40,128,128]{3,2,1,0:T(8,128)} %param.13) | copy-start | bytes 7864324
  80.2 2.8 %copy-start.6 = (s32[1,40]{1,0:T(1,128)S(1)}, s32[1,40]{1,0:T(1,128)}, u32[]{:S(2)}) copy-start(s32[1,40]{1,0:T(1,128)} %param.10) | copy-start | bytes 484
  83.0 1.8 copy-start.4
  85.6 177.0 %all-gather.7.cloned.1.call-start = ((), (), s32[]{:S(2)}) async-start(), calls=%async_computation.1 | async-start | bytes 1310720 | tf_op jit(solution)/shard_map/all_gather | solution.py:41
  142.0 57.2 %copy-start.3 = (bf16[1024,128]{1,0:T(8,128)(2,1)}, bf16[1024,128]{1,0:T(8,128)(2,1)S(1)}, u32[]{:S(2)}) copy-start(bf16[1024,128]{1,0:T(8,128)(2,1)S(1)} %get-tuple-element.5) | copy-start | bytes 786436
  156.2 20.4 %collective-permute-start.4 = (bf16[1024,128]{1,0:T(8,128)(2,1)S(1)}, bf16[1024,128]{1,0:T(8,128)(2,1)S(1)}, u32[]{:S(2)}, u32[]{:S(2)}) collective-permute-start(bf16[1024,128]{1,0:T(8,128)(2,1)S(1)} %fusion.7), channel_id=1, source_target_pairs={{0,4},{4,8},{8,12},{12,16},{16,20},{20,24},{24,28},{28,32},{32,36}... | collective-permute-start | bytes 786440 | tf_op jit(solution)/shard_map/ppermute | solution.py:20
  159.3 19.2 %collective-permute-start.6 = (bf16[1024,128]{1,0:T(8,128)(2,1)S(1)}, bf16[1024,128]{1,0:T(8,128)(2,1)S(1)}, u32[]{:S(2)}, u32[]{:S(2)}) collective-permute-start(bf16[1024,128]{1,0:T(8,128)(2,1)S(1)} %fusion.7), channel_id=1, source_target_pairs={{0,508},{4,0},{8,4},{12,8},{16,12},{20,16},{24,20},{28,24},{32,28}... | collective-permute-start | bytes 786440 | tf_op jit(solution)/shard_map/ppermute | solution.py:20
  176.6 19.5 %collective-permute-start.5 = (bf16[1024,128]{1,0:T(8,128)(2,1)S(1)}, bf16[1024,128]{1,0:T(8,128)(2,1)S(1)}, u32[]{:S(2)}, u32[]{:S(2)}) collective-permute-start(bf16[1024,128]{1,0:T(8,128)(2,1)S(1)} %collective-permute-done.4), channel_id=1, source_target_pairs={{0,4},{4,8},{8,12},{12,16},{16,20},{20,24},{24,28},{28,32},{32,36}... | collective-permute-start | bytes 786440 | tf_op jit(solution)/shard_map/ppermute | solution.py:20
  178.6 20.6 %collective-permute-start.7 = (bf16[1024,128]{1,0:T(8,128)(2,1)S(1)}, bf16[1024,128]{1,0:T(8,128)(2,1)S(1)}, u32[]{:S(2)}, u32[]{:S(2)}) collective-permute-start(bf16[1024,128]{1,0:T(8,128)(2,1)S(1)} %collective-permute-done.6), channel_id=1, source_target_pairs={{0,508},{4,0},{8,4},{12,8},{16,12},{20,16},{24,20},{28,24},{32,28}... | collective-permute-start | bytes 786440 | tf_op jit(solution)/shard_map/ppermute | solution.py:20
  208.7 1.0 copy-start.5
Sparse Core Ops, SparseCore 0:
  85.7 54.4 all-gather.4
  210.6 51.9 all-gather.6
